TPU v7x, 32 devices: a whole 2x2x4 slice. The times are simulated.
32 devices in a mesh: seq: 8 (over y, x, core), tp: 4 (over z).
Axes of the slice: x: 2, y: 2, z: 4, core: 2. Of those that a mesh axis runs over, the one named last changes fastest.
Arguments:
- inputs: bfloat16 [16384, 1024], P(('seq', 'tp')), may hold values from -6 to 6
- segment_ids: int32 [8, 2048], P('seq'), may hold values from 0 to 5, never falling along the last dimension, each value on 1 to 512 neighbouring positions
- row_lengths: int32 [8], P('seq'), may hold values from 1536 to 2048
- norm1_gain: float32 [1024], replicated, may hold values from 0.5 to 1.5
- norm1_shift: float32 [1024], replicated, may hold values from -4 to 4
- w_query: bfloat16 [1024, 1024], P(None, 'tp'), may hold values from -0.1875 to 0.1875
- w_key: bfloat16 [1024, 1024], P(None, 'tp'), may hold values from -0.1875 to 0.1875
- w_value: bfloat16 [1024, 1024], P(None, 'tp'), may hold values from -0.1875 to 0.1875
- b_query: float32 [1024], P('tp'), may hold values from -6 to 6
- b_value: float32 [1024], P('tp'), may hold values from -6 to 6
- w_out: bfloat16 [1024, 1024], P('tp'), may hold values from -2 to 2
- b_out: float32 [1024], replicated, may hold values from -6 to 6
- norm2_gain: float32 [1024], replicated, may hold values from 0.5 to 1.5
- norm2_shift: float32 [1024], replicated, may hold values from -4 to 4
- w_up: bfloat16 [1024, 1024], P(None, 'tp'), may hold values from -0.1875 to 0.1875
- b_up: float32 [1024], P('tp'), may hold values from -6 to 6
- w_down: bfloat16 [1024, 1024], P('tp'), may hold values from -0.1875 to 0.1875
- b_down: float32 [1024], replicated, may hold values from -6 to 6
- out_grad: bfloat16 [16384, 1024], P(('seq', 'tp')), may hold values from -6 to 6
Outputs:
- output: bfloat16 [16384, 1024], P(('seq', 'tp'))
- grad_inputs: bfloat16 [16384, 1024], P(('seq', 'tp'))
- grad_norm1_gain: float32 [1024], replicated
- grad_norm1_shift: float32 [1024], replicated
- grad_w_query: float32 [1024, 1024], P(None, 'tp')
- grad_w_key: float32 [1024, 1024], P(None, 'tp')
- grad_w_value: float32 [1024, 1024], P(None, 'tp')
- grad_b_query: float32 [1024], P('tp')
- grad_b_value: float32 [1024], P('tp')
- grad_w_out: float32 [1024, 1024], P('tp')
- grad_b_out: float32 [1024], replicated
- grad_norm2_gain: float32 [1024], replicated
- grad_norm2_shift: float32 [1024], replicated
- grad_w_up: float32 [1024, 1024], P(None, 'tp')
- grad_b_up: float32 [1024], P('tp')
- grad_w_down: float32 [1024, 1024], P('tp')
- grad_b_down: float32 [1024], replicated
Inputs may be any that keep to these rules, and one draw needn't show every extreme that they name: `segment_ids`: along a row segment numbers never fall, and one number covers at most 512 positions; positions at or past a row's length are padding.
All inputs are finite; a program needn't handle non-finite values.
Results may differ from a plain program's by a relative error of at most 0.018.
Values may be sent and summed in bfloat16 or wider, within the bound.
No kernel may reach another device: no remote copies, remote signals or barrier semaphores. Data moves between devices by JAX's collectives and lax.ppermute only.
A program may use at most 128 MiB of HBM per device.

v0:
```python
import jax
import jax.numpy as jnp
from jax import lax
from jax.sharding import PartitionSpec as P

HEAD_DIM = 128
ROW_LEN = 2048


norm_eps = 1e-05
mask_fill = -1000000000.0


def norm_rows(values, gain_vec, shift_vec):
    centre = values - jnp.mean(values, axis=-1, keepdims=True)
    spread = jnp.mean(centre * centre, axis=-1, keepdims=True)
    return centre * lax.rsqrt(spread + norm_eps) * gain_vec + shift_vec


def gelu_exact(values):
    return jax.nn.gelu(values, approximate=False)


def across_rows(left, right):
    return lax.dot_general(
        left, right, (((0,), (0,)), ((), ())), preferred_element_type=jnp.float32
    )


def against_cols(left, right):
    return lax.dot_general(
        left, right, (((1,), (1,)), ((), ())), preferred_element_type=jnp.float32
    )


def allowed_block(seg_row, row_length, query_start, block_rows):
    key_pos = jnp.arange(ROW_LEN, dtype=jnp.int32)
    query_pos = query_start + jnp.arange(block_rows, dtype=jnp.int32)
    query_seg = lax.dynamic_slice_in_dim(seg_row, query_start, block_rows, 0)
    same_image = query_seg[:, None] == seg_row[None, :]
    both_inside = (query_pos < row_length)[:, None] & (key_pos < row_length)[None, :]
    itself = query_pos[:, None] == key_pos[None, :]
    return same_image & (both_inside | itself)


def body(
    inputs,
    segment_ids,
    row_lengths,
    norm1_gain,
    norm1_shift,
    w_query,
    w_key,
    w_value,
    b_query,
    b_value,
    w_out,
    b_out,
    norm2_gain,
    norm2_shift,
    w_up,
    b_up,
    w_down,
    b_down,
    out_grad,
):
    width_local = w_query.shape[1]
    heads_local = width_local // HEAD_DIM
    rows_here = segment_ids.shape[0]
    block_rows = min(512, ROW_LEN)
    blocks_per_row = ROW_LEN // block_rows
    scale = HEAD_DIM ** (-0.5)
    gathered_rows = rows_here * ROW_LEN
    head_shape = (gathered_rows, heads_local, HEAD_DIM)
    wide_in = inputs.astype(jnp.float32)
    normed_first, pull_first = jax.vjp(norm_rows, wide_in, norm1_gain, norm1_shift)
    first_all = lax.all_gather(normed_first.astype(jnp.bfloat16), "tp", axis=0, tiled=True)
    proj_weight = jnp.concatenate([w_query, w_key, w_value], axis=1)
    proj_bias = jnp.concatenate([b_query, jnp.zeros_like(b_query), b_value])
    projected = (
        jnp.dot(first_all, proj_weight, preferred_element_type=jnp.float32) + proj_bias
    ).astype(jnp.bfloat16)
    query_heads = projected[:, :width_local].reshape(head_shape)
    key_heads = projected[:, width_local : 2 * width_local].reshape(head_shape)
    value_heads = projected[:, 2 * width_local :].reshape(head_shape)

    def attend_block(flat_index):
        row_index = flat_index // blocks_per_row
        query_start = flat_index % blocks_per_row * block_rows
        seg_row = lax.dynamic_index_in_dim(segment_ids, row_index, 0, keepdims=False)
        row_length = lax.dynamic_index_in_dim(row_lengths, row_index, 0, keepdims=False)
        allowed = allowed_block(seg_row, row_length, query_start, block_rows)
        query_blk = lax.dynamic_slice_in_dim(
            query_heads, row_index * ROW_LEN + query_start, block_rows, 0
        )
        scores = (
            jnp.einsum("qhe,khe->hqk", query_blk, key_heads, preferred_element_type=jnp.float32)
            * scale
        )
        scores = jnp.where(allowed[None], scores, mask_fill)
        top_score = jnp.max(scores, axis=-1, keepdims=True)
        raised = jnp.exp(scores - top_score)
        row_total = jnp.sum(raised, axis=-1, keepdims=True)
        probs_low = (raised / row_total).astype(jnp.bfloat16)
        mixed_blk = jnp.einsum(
            "hqk,khe->qhe", probs_low, value_heads, preferred_element_type=jnp.float32
        )
        log_total = (top_score + jnp.log(row_total))[:, :, 0]
        return (mixed_blk.astype(jnp.bfloat16), log_total)

    mixed_all, log_totals = lax.map(
        attend_block, jnp.arange(rows_here * blocks_per_row, dtype=jnp.int32)
    )
    mixed_flat = mixed_all.reshape(gathered_rows, width_local)
    attn_sum = lax.psum_scatter(
        jnp.dot(mixed_flat, w_out, preferred_element_type=jnp.float32).astype(jnp.bfloat16),
        "tp",
        scatter_dimension=0,
        tiled=True,
    ).astype(jnp.float32)
    first_resid = wide_in + attn_sum + b_out
    normed_second, pull_second = jax.vjp(norm_rows, first_resid, norm2_gain, norm2_shift)
    second_all = lax.all_gather(normed_second.astype(jnp.bfloat16), "tp", axis=0, tiled=True)
    up_act = jnp.dot(second_all, w_up, preferred_element_type=jnp.float32) + b_up
    hidden_act, pull_gelu = jax.vjp(gelu_exact, up_act)
    hidden_low = hidden_act.astype(jnp.bfloat16)
    mlp_sum = lax.psum_scatter(
        jnp.dot(hidden_low, w_down, preferred_element_type=jnp.float32).astype(jnp.bfloat16),
        "tp",
        scatter_dimension=0,
        tiled=True,
    ).astype(jnp.float32)
    output = (first_resid + mlp_sum + b_down).astype(jnp.bfloat16)
    grad_out = out_grad.astype(jnp.float32)
    grad_b_down = jnp.sum(grad_out, axis=0)
    cotangent_all = lax.all_gather(out_grad, "tp", axis=0, tiled=True)
    grad_w_down = across_rows(hidden_low, cotangent_all)
    grad_hidden = against_cols(cotangent_all, w_down)
    grad_up = pull_gelu(grad_hidden)[0].astype(jnp.bfloat16)
    grad_b_up = jnp.sum(grad_up.astype(jnp.float32), axis=0)
    grad_second = lax.psum_scatter(
        against_cols(grad_up, w_up).astype(jnp.bfloat16), "tp", scatter_dimension=0, tiled=True
    ).astype(jnp.float32)
    grad_resid_norm, grad_norm2_gain, grad_norm2_shift = pull_second(grad_second)
    grad_resid = grad_out + grad_resid_norm
    grad_b_out = jnp.sum(grad_resid, axis=0)
    resid_all = lax.all_gather(grad_resid.astype(jnp.bfloat16), "tp", axis=0, tiled=True)
    grad_w_out = across_rows(mixed_flat, resid_all)
    grad_mixed = against_cols(resid_all, w_out).astype(jnp.bfloat16).reshape(head_shape)

    def back_row(row_index):
        seg_row = lax.dynamic_index_in_dim(segment_ids, row_index, 0, keepdims=False)
        row_length = lax.dynamic_index_in_dim(row_lengths, row_index, 0, keepdims=False)

        def back_block(carry_grads, block_index):
            grad_keys, grad_values = carry_grads
            query_start = block_index * block_rows
            start_row = row_index * ROW_LEN + query_start
            query_blk = lax.dynamic_slice_in_dim(query_heads, start_row, block_rows, 0)
            grad_blk = lax.dynamic_slice_in_dim(grad_mixed, start_row, block_rows, 0)
            log_total = lax.dynamic_index_in_dim(
                log_totals, row_index * blocks_per_row + block_index, 0, keepdims=False
            )
            allowed = allowed_block(seg_row, row_length, query_start, block_rows)
            scores = (
                jnp.einsum("qhe,khe->hqk", query_blk, key_heads, preferred_element_type=jnp.float32)
                * scale
            )
            scores = jnp.where(allowed[None], scores, mask_fill)
            attn_probs = jnp.exp(scores - log_total[:, :, None])
            probs_low = attn_probs.astype(jnp.bfloat16)
            grad_probs = jnp.einsum(
                "qhe,khe->hqk", grad_blk, value_heads, preferred_element_type=jnp.float32
            )
            weighted_mean = jnp.sum(attn_probs * grad_probs, axis=-1, keepdims=True)
            grad_scores = (attn_probs * (grad_probs - weighted_mean)).astype(jnp.bfloat16)
            grad_query_blk = (
                jnp.einsum(
                    "hqk,khe->qhe", grad_scores, key_heads, preferred_element_type=jnp.float32
                )
                * scale
            ).astype(jnp.bfloat16)
            grad_keys = (
                grad_keys
                + jnp.einsum(
                    "hqk,qhe->khe", grad_scores, query_blk, preferred_element_type=jnp.float32
                )
                * scale
            )
            grad_values = grad_values + jnp.einsum(
                "hqk,qhe->khe", probs_low, grad_blk, preferred_element_type=jnp.float32
            )
            return ((grad_keys, grad_values), grad_query_blk)

        zero_heads = jnp.zeros((ROW_LEN, heads_local, HEAD_DIM), jnp.float32)
        (grad_keys, grad_values), grad_queries = lax.scan(
            back_block, (zero_heads, zero_heads), jnp.arange(blocks_per_row, dtype=jnp.int32)
        )
        return (
            grad_queries.reshape(ROW_LEN, width_local),
            grad_keys.astype(jnp.bfloat16).reshape(ROW_LEN, width_local),
            grad_values.astype(jnp.bfloat16).reshape(ROW_LEN, width_local),
        )

    query_grads, key_grads, value_grads = lax.map(back_row, jnp.arange(rows_here, dtype=jnp.int32))
    grad_proj = jnp.concatenate(
        [
            query_grads.reshape(gathered_rows, width_local),
            key_grads.reshape(gathered_rows, width_local),
            value_grads.reshape(gathered_rows, width_local),
        ],
        axis=1,
    )
    grad_b_query = jnp.sum(query_grads.astype(jnp.float32), axis=(0, 1))
    grad_b_value = jnp.sum(value_grads.astype(jnp.float32), axis=(0, 1))
    grad_first = lax.psum_scatter(
        against_cols(grad_proj, proj_weight).astype(jnp.bfloat16),
        "tp",
        scatter_dimension=0,
        tiled=True,
    ).astype(jnp.float32)
    grad_in_norm, grad_norm1_gain, grad_norm1_shift = pull_first(grad_first)
    grad_inputs = (grad_resid + grad_in_norm).astype(jnp.bfloat16)
    grad_proj_weight = across_rows(first_all, grad_proj)
    grad_w_up = across_rows(second_all, grad_up)
    grad_w_query = grad_proj_weight[:, :width_local]
    grad_w_key = grad_proj_weight[:, width_local : 2 * width_local]
    grad_w_value = grad_proj_weight[:, 2 * width_local :]
    (
        grad_w_query,
        grad_w_key,
        grad_w_value,
        grad_b_query,
        grad_b_value,
        grad_w_out,
        grad_w_up,
        grad_b_up,
        grad_w_down,
    ) = lax.psum(
        (
            grad_w_query,
            grad_w_key,
            grad_w_value,
            grad_b_query,
            grad_b_value,
            grad_w_out,
            grad_w_up,
            grad_b_up,
            grad_w_down,
        ),
        "seq",
    )
    (
        grad_norm1_gain,
        grad_norm1_shift,
        grad_norm2_gain,
        grad_norm2_shift,
        grad_b_out,
        grad_b_down,
    ) = lax.psum(
        (
            grad_norm1_gain,
            grad_norm1_shift,
            grad_norm2_gain,
            grad_norm2_shift,
            grad_b_out,
            grad_b_down,
        ),
        ("seq", "tp"),
    )
    return (
        output,
        grad_inputs,
        grad_norm1_gain,
        grad_norm1_shift,
        grad_w_query,
        grad_w_key,
        grad_w_value,
        grad_b_query,
        grad_b_value,
        grad_w_out,
        grad_b_out,
        grad_norm2_gain,
        grad_norm2_shift,
        grad_w_up,
        grad_b_up,
        grad_w_down,
        grad_b_down,
    )


def solution(mesh):
    in_specs = (
        P(("seq", "tp"), None),
        P("seq", None),
        P("seq"),
        P(),
        P(),
        P(None, "tp"),
        P(None, "tp"),
        P(None, "tp"),
        P("tp"),
        P("tp"),
        P("tp", None),
        P(),
        P(),
        P(),
        P(None, "tp"),
        P("tp"),
        P("tp", None),
        P(),
        P(("seq", "tp"), None),
    )
    out_specs = (
        P(("seq", "tp"), None),
        P(("seq", "tp"), None),
        P(),
        P(),
        P(None, "tp"),
        P(None, "tp"),
        P(None, "tp"),
        P("tp"),
        P("tp"),
        P("tp", None),
        P(),
        P(),
        P(),
        P(None, "tp"),
        P("tp"),
        P("tp", None),
        P(),
    )
    return jax.shard_map(body, mesh=mesh, in_specs=in_specs, out_specs=out_specs, check_vma=False)
```

profile of v0, /device:TPU:0, one launch (start us, length us, event | category | flops | bytes accessed | tf_op | source)
XLA Modules:
  0.0 1004.4 jit_solution(5229092477112862982)
XLA Ops:
  16.0 80.8 %all-gather.5.cloned.1.call-done = bf16[2048,1024]{1,0:T(8,128)(2,1)} async-done(((bf16[512,1024]{1,0:T(8,128)(2,1)}), bf16[2048,1024]{1,0:T(8,128)(2,1)}) %all-gather.5.cloned.1.call-update) | async-done | bytes 4194320 | tf_op jit(solution)/shard_map/all_gather | solution.py:77
  96.8 6.1 add_convert_fusion
  106.4 2.3 copy.48
  108.6 2.3 copy.47
  110.9 64.4 %while.43 = (s32[]{:T(128)}, bf16[4,512,2,128]{3,2,1,0:T(2,128)(2,1)}, f32[4,2,512]{2,1,0:T(2,128)S(1)}, s32[4]{0:T(128)S(1)}, s32[1,2048]{1,0:T(1,128)S(1)}, /*...) while((s32[]{:T(128)}, ...), condition=%wide.region_5.6_spmd, body=%wide.region_2.5_spmd.sunk | while | flops 1104284160 | bytes 32562676 | solution.py:111
  117.3 3.3 fusion.133
  120.6 2.5 fusion.134
  123.1 2.9 fusion.135
  133.4 3.3 fusion.133
  136.7 2.5 fusion.134
  139.2 2.9 fusion.135
  149.5 3.3 fusion.133
  152.8 2.5 fusion.134
  155.3 2.9 fusion.135
  165.6 3.3 fusion.133
  168.9 2.5 fusion.134
  171.4 2.9 fusion.135
  175.3 4.5 convolution_convert_fusion.2
  180.2 75.0 %reduce-scatter.5.cloned.1.call-done = bf16[512,1024]{1,0:T(8,128)(2,1)} async-done(((bf16[2048,1024]{1,0:T(8,128)(2,1)}), bf16[512,1024]{1,0:T(8,128)(2,1)}) %reduce-scatter.5.cloned.1.call-update) | async-done | bytes 1048592 | tf_op jit(solution)/shard_map/reduce_scatter | solution.py:115
  259.8 80.8 %all-gather.7.cloned.1.call-done = bf16[2048,1024]{1,0:T(8,128)(2,1)} async-done(((bf16[512,1024]{1,0:T(8,128)(2,1)}), bf16[2048,1024]{1,0:T(8,128)(2,1)}) %all-gather.7.cloned.1.call-update) | async-done | bytes 4194320 | tf_op jit(solution)/shard_map/all_gather | solution.py:123
  340.6 4.8 convolution_add_fusion
  345.4 76.0 %all-gather.9.cloned.1.call-done = bf16[2048,1024]{1,0:T(8,128)(2,1)} async-done(((bf16[512,1024]{1,0:T(8,128)(2,1)}), bf16[2048,1024]{1,0:T(8,128)(2,1)}) %all-gather.9.cloned.1.call-update) | async-done | bytes 4194320 | tf_op jit(solution)/shard_map/all_gather | solution.py:136
  421.4 9.3 convert_reduce_fusion.4
  431.7 3.2 convolution_convert_fusion
  435.0 2.5 multiply_convert_fusion.1
  438.5 3.2 convolution_convert_fusion.1
  441.7 68.6 %reduce-scatter.9.cloned.1.call-done = bf16[512,1024]{1,0:T(8,128)(2,1)} async-done(((bf16[2048,1024]{1,0:T(8,128)(2,1)}), bf16[512,1024]{1,0:T(8,128)(2,1)}) %reduce-scatter.9.cloned.1.call-update) | async-done | bytes 1048592 | tf_op jit(solution)/shard_map/reduce_scatter | solution.py:141
  510.4 3.1 convert_reduce_fusion.1
  513.5 3.2 fusion.56
  516.7 73.1 %reduce-scatter.7.cloned.1.call-done = bf16[512,1024]{1,0:T(8,128)(2,1)} async-done(((bf16[2048,1024]{1,0:T(8,128)(2,1)}), bf16[512,1024]{1,0:T(8,128)(2,1)}) %reduce-scatter.7.cloned.1.call-update) | async-done | bytes 1048592 | tf_op jit(solution)/shard_map/reduce_scatter | solution.py:127
  589.8 4.5 fusion.78
  597.1 81.2 %all-gather.11.cloned.1.call-done = bf16[2048,1024]{1,0:T(8,128)(2,1)} async-done(((bf16[512,1024]{1,0:T(8,128)(2,1)}), bf16[2048,1024]{1,0:T(8,128)(2,1)}) %all-gather.11.cloned.1.call-update) | async-done | bytes 4194320 | tf_op jit(solution)/shard_map/all_gather | solution.py:147
  678.3 4.4 convolution_convert_fusion.4
  682.7 103.0 %while.44 = (s32[]{:T(128)}, f32[2048,2,128]{0,2,1:T(8,128)}, f32[2048,2,128]{0,2,1:T(8,128)}, bf16[4,512,2,128]{3,1,2,0:T(8,128)(2,1)}, s32[4]{0:T(128)S(1)}, /...) while((s32[]{:T(128)}, f32[2048,2,128]{0,2,1:T(8,128)}, ...), condition=%wide.region_15.16_spmd.clone, body=%wide.region_13.15_spmd.clone.sunk | while | flops 2723940864 | bytes 105172400 | solution.py:196
  689.2 2.6 fusion.145
  691.9 3.7 fusion.148
  695.6 3.8 multiply_reduce_fusion.3
  699.5 2.6 multiply_convert_fusion.3
  714.0 2.7 fusion.145
  716.7 4.9 fusion.148
  721.6 3.9 multiply_reduce_fusion.3
  725.5 2.6 multiply_convert_fusion.3
  730.1 2.2 fusion.147
  740.1 2.6 fusion.145
  742.8 4.9 fusion.148
  747.7 3.8 multiply_reduce_fusion.3
  751.5 2.6 multiply_convert_fusion.3
  766.1 2.7 fusion.145
  768.8 4.9 fusion.148
  773.7 3.9 multiply_reduce_fusion.3
  777.6 2.6 multiply_convert_fusion.3
  782.2 2.2 fusion.147
  788.8 2.3 copy.55
  795.5 7.8 convolution_convert_fusion.3
  804.5 4.6 fusion.82
  809.1 2.3 fusion.81
  812.6 3.5 fusion.66
  819.8 2.3 fusion.67
  823.6 15.3 %all-reduce.1 = (f32[256]{0:T(256)}, f32[256]{0:T(256)}, f32[256]{0:T(256)}) all-reduce(f32[256]{0:T(256)S(1)} %bitcast.127, f32[256]{0:T(256)S(1)} %bitcast.126, f32[256]{0:T(256)S(1)} %copy-done.51), channel_id=1, replica_groups=mesh['seq'=8,'tp'=4] {'seq'}, use_global_device_ids=true, to_apply=%region_27.28 | all-reduce | flops 768 | bytes 6144 | tf_op jit(solution)/shard_map/psum | solution.py:239
  838.9 39.8 %reduce-scatter.11.cloned.1.call-done = bf16[512,1024]{1,0:T(8,128)(2,1)} async-done(((bf16[2048,1024]{1,0:T(8,128)(2,1)}), bf16[512,1024]{1,0:T(8,128)(2,1)}) %reduce-scatter.11.cloned.1.call-update) | async-done | bytes 1048592 | tf_op jit(solution)/shard_map/reduce_scatter | solution.py:216
  882.0 41.7 %all-reduce = (f32[1024]{0:T(1024)}, f32[1024]{0:T(1024)}, f32[1024]{0:T(1024)}, f32[1024]{0:T(1024)}, f32[1024]{0:T(1024)}, /*index=5*/f32[1024]{0:T(1024)}) all-reduce(f32[1024]{0:T(1024)S(1)} %get-tuple-element.445, f32[1024]{0:T(1024)S(1)} %get-tuple-element.449, ...), channel_id=1, replica_groups=mesh['seq'=8,'tp'=4] {'seq','tp'}, use_global_device_ids=true, to_apply=%region_20.21 | all-reduce | flops 6144 | bytes 49152 | tf_op jit(solution)/shard_map/psum | solution.py:260
  923.7 3.6 add_convert_fusion.1
  927.3 62.9 %all-reduce.5.cloned.1.call-done = (f32[1024,256]{1,0:T(8,128)}, f32[1024,256]{1,0:T(8,128)}, f32[1024,256]{1,0:T(8,128)}, f32[256,1024]{1,0:T(8,128)}, f32[1024,256]{1,0:T(8,128)}, /*index=5*/f32[256,1024]{1,0:T(8,128)}) async-done(((f32[1024,256]{1,0:T(8,128)}, f32[1024,256]{1,0:T(8,128)}, f32[1024,256]{1,0:T(8,128)}, f32[256,1024]{1,0:T(8,128)}, f32[1024,256]{1,0:T(8,128)}, ...) | async-done | bytes 6291472 | tf_op jit(solution)/shard_map/psum | solution.py:239
  990.2 2.4 copy.112
  (263 shorter events, 96.9 us)
Async XLA Ops:
  7.2 414.3 %copy-start = (bf16[256,1024]{1,0:T(8,128)(2,1)S(1)}, bf16[256,1024]{1,0:T(8,128)(2,1)}, u32[]{:S(2)}) copy-start(bf16[256,1024]{1,0:T(8,128)(2,1)} %param.39) | copy-start | bytes 1572868
  7.2 4.6 copy-start.2
  7.2 4.5 copy-start.36
  7.2 4.5 copy-start.46
  7.2 89.6 %all-gather.5.cloned.1.call-start = ((), (), s32[]{:S(2)}) async-start(), calls=%async_computation.4 | async-start | bytes 5242880 | tf_op jit(solution)/shard_map/all_gather | solution.py:77
  8.8 2.3 copy-start.33
  8.8 4.5 copy-start.49
  8.9 4.5 copy-start.50
  8.9 4.5 copy-start.29
  11.8 2.4 copy-start.30
  13.2 1.9 copy-start.31
  13.2 242.0 %reduce-scatter.5.cloned.1.call-start = ((), (), s32[]{:S(2)}) async-start(), calls=%async_computation.5 | async-start | bytes 5242880 | tf_op jit(solution)/shard_map/reduce_scatter | solution.py:115
  106.3 4.5 copy-start.17
  110.9 64.4 %copy-start.27 = (bf16[256,1024]{1,0:T(8,128)(2,1)S(1)}, bf16[256,1024]{1,0:T(8,128)(2,1)}, u32[]{:S(2)}) copy-start(bf16[256,1024]{1,0:T(8,128)(2,1)} %param.33) | copy-start | bytes 1572868
  179.7 75.5 %copy-start.32 = (f32[1024]{0:T(1024)S(1)}, f32[1024]{0:T(1024)}, u32[]{:S(2)}) copy-start(f32[1024]{0:T(1024)} %param.34) | copy-start | bytes 12292
  179.8 77.8 %copy-start.35 = (f32[1024]{0:T(1024)S(1)}, f32[1024]{0:T(1024)}, u32[]{:S(2)}) copy-start(f32[1024]{0:T(1024)} %param.35) | copy-start | bytes 12292
  179.8 77.8 %copy-start.47 = (f32[1024]{0:T(1024)S(1)}, f32[1024]{0:T(1024)}, u32[]{:S(2)}) copy-start(f32[1024]{0:T(1024)} %param.36) | copy-start | bytes 12292
  179.8 160.8 %all-gather.7.cloned.1.call-start = ((), (), s32[]{:S(2)}) async-start(), calls=%async_computation.6 | async-start | bytes 5242880 | tf_op jit(solution)/shard_map/all_gather | solution.py:123
  257.6 83.0 %copy-start.26 = (bf16[1024,256]{1,0:T(8,128)(2,1)S(1)}, bf16[1024,256]{1,0:T(8,128)(2,1)}, u32[]{:S(2)}) copy-start(bf16[1024,256]{1,0:T(8,128)(2,1)} %param.37) | copy-start | bytes 1572868
  257.6 83.0 %copy-start.55 = (f32[256]{0:T(256)S(1)}, f32[256]{0:T(256)}, u32[]{:S(2)}) copy-start(f32[256]{0:T(256)} %param.38) | copy-start | bytes 3076
  259.2 162.2 %all-gather.9.cloned.1.call-start = ((), (), s32[]{:S(2)}) async-start(), calls=%async_computation.8 | async-start | bytes 5242880 | tf_op jit(solution)/shard_map/all_gather | solution.py:136
  259.8 250.6 %reduce-scatter.9.cloned.1.call-start = ((), (), s32[]{:S(2)}) async-start(), calls=%async_computation.9 | async-start | bytes 5242880 | tf_op jit(solution)/shard_map/reduce_scatter | solution.py:141
  434.9 154.9 %reduce-scatter.7.cloned.1.call-start = ((), (), s32[]{:S(2)}) async-start(), calls=%async_computation.7 | async-start | bytes 5242880 | tf_op jit(solution)/shard_map/reduce_scatter | solution.py:127
  441.7 236.6 %all-gather.11.cloned.1.call-start = ((), (), s32[]{:S(2)}) async-start(), calls=%async_computation.10 | async-start | bytes 5242880 | tf_op jit(solution)/shard_map/all_gather | solution.py:147
  510.4 3.1 copy-start.8
  513.5 76.3 %copy-start.48 = (f32[1024]{0:T(1024)S(1)}, f32[1024]{0:T(1024)}, u32[]{:S(2)}) copy-start(f32[1024]{0:T(1024)} %param.40) | copy-start | bytes 12292
  595.7 82.6 %copy-start.28 = (bf16[256,1024]{1,0:T(8,128)(2,1)S(1)}, bf16[256,1024]{1,0:T(8,128)(2,1)}, u32[]{:S(2)}) copy-start(bf16[256,1024]{1,0:T(8,128)(2,1)} %param.33) | copy-start | bytes 1572868
  596.8 281.9 %reduce-scatter.11.cloned.1.call-start = ((), (), s32[]{:S(2)}) async-start(), calls=%async_computation.11 | async-start | bytes 5242880 | tf_op jit(solution)/shard_map/reduce_scatter | solution.py:216
  689.2 2.7 copy-start.16
  699.4 2.6 copy-start.5
  702.1 2.0 copy-start.3
  714.0 2.7 copy-start.16
  725.5 2.6 copy-start.5
  728.1 2.0 copy-start.3
  740.1 2.7 copy-start.16
  751.5 2.6 copy-start.5
  754.1 2.0 copy-start.3
  766.1 2.7 copy-start.16
  777.6 2.6 copy-start.5
  780.2 2.0 copy-start.3
  803.3 186.9 %all-reduce.5.cloned.1.call-start = ((), (), s32[]{:S(2)}) async-start(), calls=%async_computation.12 | async-start | bytes 12582912 | tf_op jit(solution)/shard_map/psum | solution.py:239
  804.5 4.6 copy-start.14
  804.5 4.6 copy-start.53
  809.1 2.3 copy-start.23
  809.1 2.3 copy-start.24
  809.1 2.3 copy-start.25
  809.1 3.5 copy-start.52
  816.1 1.8 copy-start.15
  816.1 3.7 copy-start.54
  822.1 56.7 %copy-start.34 = (f32[512]{0:T(512)S(1)}, f32[512]{0:T(512)}, u32[]{:S(2)}) copy-start(f32[512]{0:T(512)} %copy-done.33) | copy-start | bytes 6148
  822.1 56.7 %copy-start.37 = (f32[1024]{0:T(1024)S(1)}, f32[1024]{0:T(1024)}, u32[]{:S(2)}) copy-start(f32[1024]{0:T(1024)} %param.26) | copy-start | bytes 12292
  823.3 57.4 %copy-start.41 = (f32[512]{0:T(512)S(1)}, f32[512]{0:T(512)}, u32[]{:S(2)}) copy-start(f32[512]{0:T(512)} %copy-done.40) | copy-start | bytes 6148
  823.3 57.4 %copy-start.39 = (f32[512]{0:T(512)S(1)}, f32[512]{0:T(512)}, u32[]{:S(2)}) copy-start(f32[512]{0:T(512)} %copy-done.38) | copy-start | bytes 6148
  838.9 43.1 %copy-start.42 = (f32[1024]{0:T(1024)S(1)}, f32[1024]{0:T(1024)}, u32[]{:S(2)}) copy-start(f32[1024]{0:T(1024)} %get-tuple-element.447) | copy-start | bytes 12292
  838.9 43.1 %copy-start.43 = (f32[1024]{0:T(1024)S(1)}, f32[1024]{0:T(1024)}, u32[]{:S(2)}) copy-start(f32[1024]{0:T(1024)} %get-tuple-element.443) | copy-start | bytes 12292
  838.9 43.1 %copy-start.44 = (f32[1024]{0:T(1024)S(1)}, f32[1024]{0:T(1024)}, u32[]{:S(2)}) copy-start(f32[1024]{0:T(1024)} %get-tuple-element.513) | copy-start | bytes 12292
  838.9 43.1 %copy-start.45 = (f32[1024]{0:T(1024)S(1)}, f32[1024]{0:T(1024)}, u32[]{:S(2)}) copy-start(f32[1024]{0:T(1024)} %get-tuple-element.526) | copy-start | bytes 12292
  878.7 2.0 copy-start.9
  990.2 2.4 copy-start.22
  990.2 3.4 copy-start.21
  992.6 1.9 copy-start.20
  993.5 2.0 copy-start.19
  994.5 1.9 copy-start.18
  994.5 2.9 copy-start.1
  (13 other events, 15.6 us)
Sparse Core Ops, SparseCore 0:
  13.3 83.4 all-gather.4
  179.9 75.2 reduce-scatter.4
  259.3 81.2 all-gather.6
  342.1 79.2 all-gather.8
  435.0 75.2 reduce-scatter.8
  512.5 77.2 reduce-scatter.6
  597.0 81.2 all-gather.10
  803.4 75.2 reduce-scatter.10
  883.9 106.2 all-reduce.4
where the time goes:
time: 1020 us; the launch traced here: 1000 us
  waiting for transfers between devices  639 us (63%)
  matrix products  142 us (14%)
  other arithmetic  79.3 us (8%)
  blocking collectives  56.9 us (6%)
  local copies, waits for them, and re-layouts  50.3 us (5%)
  loops' own time  21.5 us (2%)
  between operations  14.7 us (1%)
    all_gather x1, waiting for transfers between devices, body(): lax.all_gather(grad_resid.astype(jnp.bfloat16), 'tp', axis=0, tiled=True)  81.2 us
    all_gather x1, waiting for transfers between devices, body(): lax.all_gather(normed_first.astype(jnp.bfloat16), 'tp', axis=0, tiled=True)  80.8 us
    all_gather x1, waiting for transfers between devices, body(): lax.all_gather(normed_second.astype(jnp.bfloat16), 'tp', axis=0, tiled=True)  80.8 us
    all_gather x1, waiting for transfers between devices, body(): cotangent_all = lax.all_gather(out_grad, 'tp', axis=0, tiled=True)  76 us
    reduce_scatter x1, waiting for transfers between devices, body(): lax.psum_scatter(jnp.dot(mixed_flat, w_out, preferred_element_type=jnp.fl...  75 us
    reduce_scatter x1, waiting for transfers between devices, body(): lax.psum_scatter(jnp.dot(hidden_low, w_down, preferred_element_type=jnp.f...  73.1 us
    reduce_scatter x1, waiting for transfers between devices, body(): lax.psum_scatter(against_cols(grad_up, w_up).astype(jnp.bfloat16), 'tp',...  68.6 us
    psum x1, waiting for transfers between devices, body(): lax.psum((grad_w_query, grad_w_key, grad_w_value, grad_b_query, grad_b_va...  62.9 us
  transfers between devices with their start and end apart: 9, of which 9 were waited for; matrix products, arithmetic and copies ran while one was open for 4% of the time, Pallas kernels for 0%

commit v1 on v0

v1 whole, which is shorter than its diff:
```python
import jax
import jax.numpy as jnp
from jax import lax
from jax.experimental import pallas as pl
from jax.experimental.pallas import tpu as pltpu
from jax.sharding import PartitionSpec as P

HEAD_DIM = 128
ROW_LEN = 2048
NORM_EPS = 1e-05
MASKED = -1000000000.0
LOG2E = 1.4426950408889634
BQ = 256
BK = 256
F32 = jnp.float32
BF16 = jnp.bfloat16
VMEM_LIMIT = 56 * 1024 * 1024


def dot_nn(a, b):
    return lax.dot_general(a, b, (((1,), (0,)), ((), ())), preferred_element_type=F32)


def dot_nt(a, b):
    return lax.dot_general(a, b, (((1,), (1,)), ((), ())), preferred_element_type=F32)


def dot_tn(a, b):
    return lax.dot_general(a, b, (((0,), (0,)), ((), ())), preferred_element_type=F32)


def normalise(x):
    centre = x - jnp.mean(x, axis=-1, keepdims=True)
    rstd = lax.rsqrt(jnp.mean(centre * centre, axis=-1, keepdims=True) + NORM_EPS)
    return centre * rstd, rstd


def norm_back(grad, hat, rstd, gain):
    t = gain * grad
    mean_t = jnp.mean(t, axis=-1, keepdims=True)
    mean_th = jnp.mean(t * hat, axis=-1, keepdims=True)
    return (t - mean_t - hat * mean_th) * rstd


def attend_kernel(rng, segq, segk, q, k, v, mixed, lse, s_scr, m_scr, l_scr, acc):
    heads = q.shape[1] // HEAD_DIM
    coef = HEAD_DIM**-0.5 * LOG2E
    for qb in range(q.shape[0] // BQ):
        rows = slice(qb * BQ, (qb + 1) * BQ)
        lo = rng[0, qb]
        hi = rng[1, qb]
        sq = segq[rows, :]
        m_scr[...] = jnp.full(m_scr.shape, -3e38, F32)
        l_scr[...] = jnp.zeros(l_scr.shape, F32)
        acc[...] = jnp.zeros(acc.shape, F32)

        @pl.loop(lo, hi)
        def _(kc):
            ks = pl.multiple_of(kc * BK, BK)
            bias = jnp.where(sq == segk[:, pl.ds(ks, BK)], 0.0, MASKED)
            for h in range(heads):
                cols = slice(h * HEAD_DIM, (h + 1) * HEAD_DIM)
                s = dot_nt(q[rows, cols], k[pl.ds(ks, BK), cols]) * coef + bias
                s_scr[kc, h] = s
                m = m_scr[h]
                for c in range(0, BK, 128):
                    m = jnp.maximum(m, s[:, c : c + 128])
                m_scr[h] = m

        for h in range(heads):
            m_scr[h] = jnp.broadcast_to(jnp.max(m_scr[h], axis=1, keepdims=True), (BQ, 128))

        @pl.loop(lo, hi)
        def _(kc):
            ks = pl.multiple_of(kc * BK, BK)
            for h in range(heads):
                cols = slice(h * HEAD_DIM, (h + 1) * HEAD_DIM)
                m = m_scr[h]
                p = jnp.exp2(s_scr[kc, h] - jnp.concatenate([m] * (BK // 128), axis=1))
                total = l_scr[h]
                for c in range(0, BK, 128):
                    total = total + p[:, c : c + 128]
                l_scr[h] = total
                acc[h] += dot_nn(p.astype(BF16), v[pl.ds(ks, BK), cols])

        for h in range(heads):
            cols = slice(h * HEAD_DIM, (h + 1) * HEAD_DIM)
            total = jnp.broadcast_to(jnp.sum(l_scr[h], axis=1, keepdims=True), (BQ, 128))
            mixed[rows, cols] = (acc[h] / total).astype(BF16)
            log_total = m_scr[h] + jnp.log2(total)
            for r in range(0, BQ, 128):
                part = jnp.transpose(log_total[r : r + 128])
                lse[h : h + 1, qb * BQ + r : qb * BQ + r + 128] = part[:1]


def attend(rng, segq, segk, q, k, v):
    tokens, width = q.shape
    window = k.shape[0]
    heads = width // HEAD_DIM
    smem = pl.BlockSpec(memory_space=pltpu.SMEM)
    vmem = pl.BlockSpec(memory_space=pltpu.VMEM)
    return pl.pallas_call(
        attend_kernel,
        out_shape=(
            jax.ShapeDtypeStruct((tokens, width), BF16),
            jax.ShapeDtypeStruct((heads, tokens), F32),
        ),
        in_specs=[smem] + [vmem] * 5,
        out_specs=(vmem, vmem),
        scratch_shapes=[
            pltpu.VMEM((window // BK, heads, BQ, BK), F32),
            pltpu.VMEM((heads, BQ, 128), F32),
            pltpu.VMEM((heads, BQ, 128), F32),
            pltpu.VMEM((heads, BQ, HEAD_DIM), F32),
        ],
        compiler_params=pltpu.CompilerParams(vmem_limit_bytes=VMEM_LIMIT),
        name="attend",
    )(rng, segq, segk, q, k, v)


def attend_back_kernel(
    rng, segq, segk, lse, delta, q, do, k, v, dq, dk, dv, dq_acc, dk_acc, dv_acc
):
    heads = q.shape[1] // HEAD_DIM
    scale = HEAD_DIM**-0.5
    coef = scale * LOG2E
    dk_acc[...] = jnp.zeros(dk_acc.shape, F32)
    dv_acc[...] = jnp.zeros(dv_acc.shape, F32)
    for qb in range(q.shape[0] // BQ):
        rows = slice(qb * BQ, (qb + 1) * BQ)
        lo = rng[0, qb]
        hi = rng[1, qb]
        sq = segq[:, rows]
        dq_acc[...] = jnp.zeros(dq_acc.shape, F32)

        @pl.loop(lo, hi)
        def _(kc):
            ks = pl.ds(pl.multiple_of(kc * BK, BK), BK)
            bias = jnp.where(segk[ks, :] == sq, 0.0, MASKED)
            for h in range(heads):
                cols = slice(h * HEAD_DIM, (h + 1) * HEAD_DIM)
                qh = q[rows, cols]
                doh = do[rows, cols]
                kh = k[ks, cols]
                s = dot_nt(kh, qh) * coef + (bias - lse[h : h + 1, rows])
                p = jnp.exp2(s)
                dp = dot_nt(v[ks, cols], doh)
                ds = (p * (dp - delta[h : h + 1, rows])).astype(BF16)
                dv_acc[ks, cols] += dot_nn(p.astype(BF16), doh)
                dk_acc[ks, cols] += dot_nn(ds, qh)
                dq_acc[:, cols] += dot_tn(ds, kh)

        dq[rows, :] = (dq_acc[...] * scale).astype(BF16)
    dk[...] = (dk_acc[...] * scale).astype(BF16)
    dv[...] = dv_acc[...].astype(BF16)


def attend_back(rng, segq, segk, lse, delta, q, do, k, v):
    tokens, width = q.shape
    window = k.shape[0]
    smem = pl.BlockSpec(memory_space=pltpu.SMEM)
    vmem = pl.BlockSpec(memory_space=pltpu.VMEM)
    return pl.pallas_call(
        attend_back_kernel,
        out_shape=(
            jax.ShapeDtypeStruct((tokens, width), BF16),
            jax.ShapeDtypeStruct((window, width), BF16),
            jax.ShapeDtypeStruct((window, width), BF16),
        ),
        in_specs=[smem] + [vmem] * 8,
        out_specs=(vmem, vmem, vmem),
        scratch_shapes=[
            pltpu.VMEM((BQ, width), F32),
            pltpu.VMEM((window, width), F32),
            pltpu.VMEM((window, width), F32),
        ],
        compiler_params=pltpu.CompilerParams(vmem_limit_bytes=VMEM_LIMIT),
        name="attend_back",
    )(rng, segq, segk, lse, delta, q, do, k, v)


def make_body(n_seq, n_tp):
    def shift(x, by):
        pairs = [(i, i + by) for i in range(n_tp) if 0 <= i + by < n_tp]
        return lax.ppermute(x, "tp", pairs)

    def gather_cols(parts):
        m = len(parts)
        rows, width = parts[0].shape
        piece = rows // n_seq
        mine = lax.axis_index("seq") * piece
        cut = jnp.concatenate([lax.dynamic_slice_in_dim(p, mine, piece, 0) for p in parts], axis=1)
        full = lax.all_gather(cut, ("seq", "tp"), axis=0)
        full = full.reshape(n_seq, n_tp, piece, m, width)
        full = jnp.transpose(full, (3, 0, 2, 1, 4)).reshape(m, rows, n_tp * width)
        return [full[i] for i in range(m)]

    def reduce_cols(grads):
        m = len(grads)
        rows, cols = grads[0].shape
        piece, width = rows // n_seq, cols // n_tp
        x = jnp.stack(grads).astype(BF16).reshape(m, n_seq, piece, n_tp, width)
        x = jnp.transpose(x, (1, 3, 2, 0, 4)).reshape(n_seq, n_tp, piece, m * width)
        x = lax.psum_scatter(x, "seq", scatter_dimension=0, tiled=True)
        x = lax.psum_scatter(x, "tp", scatter_dimension=1, tiled=True)
        x = lax.all_gather(x, "seq", axis=0, tiled=True)
        x = x.reshape(rows, m, width).astype(F32)
        return [x[:, i] for i in range(m)]

    def body(
        inputs,
        segment_ids,
        row_lengths,
        norm1_gain,
        norm1_shift,
        w_query,
        w_key,
        w_value,
        b_query,
        b_value,
        w_out,
        b_out,
        norm2_gain,
        norm2_shift,
        w_up,
        b_up,
        w_down,
        b_down,
        out_grad,
    ):
        tokens, width = inputs.shape
        halo = tokens
        heads = width // HEAD_DIM
        tp_at = lax.axis_index("tp")

        wq, wk, wv = gather_cols([w_query, w_key, w_value])
        wo_t, wup, wdn_t = gather_cols([w_out.T, w_up, w_down.T])
        wo, wdn = wo_t.T, wdn_t.T
        biases = lax.all_gather(jnp.stack([b_query, b_value, b_up]), "tp", axis=1, tiled=True)
        bq, bv, bup = biases[0], biases[1], biases[2]

        left = shift(inputs, 1)
        right = shift(inputs, -1)
        window = jnp.concatenate([left, inputs, right], axis=0)
        position = jnp.arange(ROW_LEN, dtype=jnp.int32)
        numbers = jnp.where(position < row_lengths[0], segment_ids[0], 4096 + position)
        numbers = jnp.concatenate(
            [jnp.full((halo,), -1, jnp.int32), numbers, jnp.full((halo,), 1 << 20, jnp.int32)]
        )
        seg_win = lax.dynamic_slice_in_dim(numbers, tp_at * tokens, tokens + 2 * halo, 0)
        seg_mine = seg_win[halo : halo + tokens]
        first = seg_mine[::BQ]
        last = seg_mine[BQ - 1 :: BQ]
        low = jnp.sum((seg_win[None, :] < first[:, None]).astype(jnp.int32), axis=1)
        high = jnp.sum((seg_win[None, :] <= last[:, None]).astype(jnp.int32), axis=1)
        rng = jnp.stack([low // BK, (high + BK - 1) // BK])

        wide = window.astype(F32)
        hat1, rstd1 = normalise(wide)
        first_low = (hat1 * norm1_gain + norm1_shift).astype(BF16)
        own = first_low[halo : halo + tokens]
        q = (dot_nn(own, wq) + bq).astype(BF16)
        k = dot_nn(first_low, wk).astype(BF16)
        v = (dot_nn(first_low, wv) + bv).astype(BF16)
        mixed, lse = attend(rng, seg_mine[:, None], seg_win[None, :], q, k, v)

        wide_in = wide[halo : halo + tokens]
        first_resid = wide_in + dot_nn(mixed, wo) + b_out
        hat2, rstd2 = normalise(first_resid)
        second_low = (hat2 * norm2_gain + norm2_shift).astype(BF16)
        up = dot_nn(second_low, wup) + bup
        hidden_act, pull_gelu = jax.vjp(lambda u: jax.nn.gelu(u, approximate=False), up)
        hidden = hidden_act.astype(BF16)
        output = (first_resid + dot_nn(hidden, wdn) + b_down).astype(BF16)

        grad_out = out_grad.astype(F32)
        g_wdn = dot_tn(hidden, out_grad)
        g_up = pull_gelu(dot_nt(out_grad, wdn))[0].astype(BF16)
        g_wup = dot_tn(second_low, g_up)
        g_second = dot_nt(g_up, wup)
        g_resid = grad_out + norm_back(g_second, hat2, rstd2, norm2_gain)
        resid_low = g_resid.astype(BF16)
        g_wo = dot_tn(mixed, resid_low)
        g_mixed = dot_nt(resid_low, wo).astype(BF16)
        delta = jnp.sum(
            (g_mixed.astype(F32) * mixed.astype(F32)).reshape(tokens, heads, HEAD_DIM), axis=2
        ).T
        out_wo_t, out_wup, out_wdn_t = reduce_cols([g_wo.T, g_wup, g_wdn.T])

        dq, dk, dv = attend_back(
            rng, seg_mine[None, :], seg_win[:, None], lse, delta, q, g_mixed, k, v
        )
        g_wq = dot_tn(own, dq)
        g_wk = dot_tn(first_low, dk)
        g_wv = dot_tn(first_low, dv)
        out_wq, out_wk, out_wv = reduce_cols([g_wq, g_wk, g_wv])
        dx = dot_nt(dk, wk) + dot_nt(dv, wv)
        to_left = shift(dx[:halo].astype(BF16), -1)
        to_right = shift(dx[halo + tokens :].astype(BF16), 1)
        g_first = dx[halo : halo + tokens] + dot_nt(dq, wq)
        g_first = g_first + to_left.astype(F32) + to_right.astype(F32)
        hat_own = hat1[halo : halo + tokens]
        rstd_own = rstd1[halo : halo + tokens]
        g_inputs = (g_resid + norm_back(g_first, hat_own, rstd_own, norm1_gain)).astype(BF16)

        def over_tokens(x):
            return jnp.sum(x.astype(F32), axis=0)

        vectors = jnp.stack(
            [
                over_tokens(g_first * hat_own),
                over_tokens(g_first),
                over_tokens(dq),
                over_tokens(dv),
                over_tokens(g_resid),
                over_tokens(g_second * hat2),
                over_tokens(g_second),
                over_tokens(g_up),
                over_tokens(grad_out),
            ]
        )
        vectors = lax.psum(vectors, ("seq", "tp"))
        n1g, n1s, g_bq, g_bv, g_bo, n2g, n2s, g_bup, g_bdn = [vectors[i] for i in range(9)]

        def shard(x):
            size = width // n_tp
            return lax.dynamic_slice_in_dim(x, tp_at * size, size, 0)

        return (
            output,
            g_inputs,
            n1g,
            n1s,
            out_wq,
            out_wk,
            out_wv,
            shard(g_bq),
            shard(g_bv),
            out_wo_t.T,
            g_bo,
            n2g,
            n2s,
            out_wup,
            shard(g_bup),
            out_wdn_t.T,
            g_bdn,
        )

    return body


def solution(mesh):
    tok = P(("seq", "tp"), None)
    col, row, vec, rep = P(None, "tp"), P("tp", None), P("tp"), P()
    in_specs = (
        tok, P("seq", None), P("seq"), rep, rep, col, col, col, vec, vec,
        row, rep, rep, rep, col, vec, row, rep, tok,
    )
    out_specs = (
        tok, tok, rep, rep, col, col, col, vec, vec,
        row, rep, rep, rep, col, vec, row, rep,
    )
    body = make_body(mesh.shape["seq"], mesh.shape["tp"])
    return jax.shard_map(body, mesh=mesh, in_specs=in_specs, out_specs=out_specs, check_vma=False)
```

time: 1020 us -> 591 us (0.58)
  waiting for transfers between devices: 639 us -> 168 us
  local copies, waits for them, and re-layouts: 50.3 us -> 141 us
  matrix products: 142 us -> 80.4 us
  Pallas kernels: 0 us -> 37.7 us
  other arithmetic: 79.3 us -> 41.6 us
  blocking collectives: 56.9 us -> 82.6 us
  loops' own time: 21.5 us -> 0 us
  starting transfers between devices: 0.89 us -> 13.7 us
    all_gather x4, waiting for transfers between devices: 319 us -> 63.6 us  [the longest x2 63.6 us: gather_cols(): full = lax.all_gather(cut, ('seq', 'tp'), axis=0)]
    reduce_scatter x4, waiting for transfers between devices: 257 us -> 93.4 us  [the longest x2 66.6 us: reduce_cols(): x = lax.psum_scatter(x, 'seq', scatter_dimension=0, tiled=True)]
    psum x1 -> x0, waiting for transfers between devices: 62.9 us -> none  [body(): lax.psum((grad_w_query, grad_w_key, grad_w_value, grad_b_query, grad_b_va...]
    dot_general x40 -> x18, matrix products: 142 us -> 80.4 us  [the longest x6 27.5 us: dot_nn(): lax.dot_general(a, b, (((1,), (0,)), ((), ())), preferred_element_type=F32)]
    another operation x0 -> x12, local copies, waits for them, and re-layouts: none -> 43.1 us  [the longest x11 43 us: reduce_cols(): x = jnp.stack(grads).astype(BF16).reshape(m, n_seq, piece, n_tp, width)]
    all_gather x0 -> x1, blocking collectives: none -> 42.1 us  [body(): lax.all_gather(jnp.stack([b_query, b_value, b_up]), 'tp', axis=1, tiled=T...]
    pallas_call x0 -> x2, Pallas kernels: none -> 37.7 us  [the longest x1 25.7 us: attend_back(): pl.pallas_call(attend_back_kernel, out_shape=(jax.ShapeDtypeStruct((token...]
    reshape x2 -> x3, local copies, waits for them, and re-layouts: 2.8 us -> 25.9 us  [gather_cols(): full = full.reshape(n_seq, n_tp, piece, m, width)]
  transfers between devices with their start and end apart: 9 -> 12, of which waited for: 9 -> 6; matrix products, arithmetic and copies ran while one was open for 4% -> 27% of each run, Pallas kernels for 0% -> 4%
where the time goes in v1:
time: 591 us; the launch traced here: 581 us
  waiting for transfers between devices  168 us (28%)
  local copies, waits for them, and re-layouts  141 us (24%)
  blocking collectives  82.6 us (14%)
  matrix products  80.4 us (14%)
  other arithmetic  41.6 us (7%)
  Pallas kernels  37.7 us (6%)
  between operations  15.9 us (3%)
  starting transfers between devices  13.7 us (2%)
    reduce_scatter x2, waiting for transfers between devices, reduce_cols(): x = lax.psum_scatter(x, 'seq', scatter_dimension=0, tiled=True)  66.6 us
    all_gather x2, waiting for transfers between devices, gather_cols(): full = lax.all_gather(cut, ('seq', 'tp'), axis=0)  63.6 us
    another operation x11, local copies, waits for them, and re-layouts, reduce_cols(): x = jnp.stack(grads).astype(BF16).reshape(m, n_seq, piece, n_tp, width)  43 us
    all_gather x1, blocking collectives, body(): lax.all_gather(jnp.stack([b_query, b_value, b_up]), 'tp', axis=1, tiled=T...  42.1 us
    psum x1, blocking collectives, body(): vectors = lax.psum(vectors, ('seq', 'tp'))  40.4 us
    dot_general x6, matrix products, dot_nn(): lax.dot_general(a, b, (((1,), (0,)), ((), ())), preferred_element_type=F32)  27.5 us
    dot_general x6, matrix products, dot_tn(): lax.dot_general(a, b, (((0,), (0,)), ((), ())), preferred_element_type=F32)  27 us
    reduce_scatter x2, waiting for transfers between devices, reduce_cols(): x = lax.psum_scatter(x, 'tp', scatter_dimension=1, tiled=True)  26.8 us
  transfers between devices with their start and end apart: 12, of which 6 were waited for; matrix products, arithmetic and copies ran while one was open for 27% of the time, Pallas kernels for 4%

profile of v1, /device:TPU:0, one launch (start us, length us, event | category | flops | bytes accessed | tf_op | source)
XLA Modules:
  0.0 580.8 jit_solution(7807054130999161868)
XLA Ops:
  12.5 5.0 collective-permute-start
  21.3 42.1 %all_gather.23 = f32[3,1024]{1,0:T(4,128)S(1)} all-gather(f32[3,256]{1,0:T(4,128)S(1)} %pad_maximum_fusion.5), channel_id=1, replica_groups=mesh['seq'=8,'tp'=4] {'tp'}, dimensions={1}, use_global_device_ids=true | all-gather | bytes 15360 | tf_op jit(solution)/shard_map/all_gather | solution.py:239
  66.0 3.0 multiply_reduce_fusion
  69.0 4.7 fusion.70
  73.7 5.1 subtract_multiply_fusion
  78.8 9.2 %all-gather.11.cloned.1.call-done = bf16[4096,768]{1,0:T(8,128)(2,1)} async-done(((bf16[128,768]{1,0:T(8,128)(2,1)}), bf16[4096,768]{1,0:T(8,128)(2,1)}) %all-gather.11.cloned.1.call-update) | async-done | bytes 6291472 | tf_op jit(solution)/shard_map/all_gather | solution.py:193
  88.0 8.7 %copy.101 = bf16[4096,768]{0,1:T(8,128)(2,1)} copy(bf16[4096,768]{1,0:T(8,128)(2,1)} %all-gather.11.cloned.1.call-done) | data formatting | bytes 12582912 | tf_op jit(solution)/shard_map/all_gather | solution.py:193
  96.7 11.0 %reshape.259 = bf16[8,4,128,3,256]{2,1,0,4,3:T(4,128)(2,1)} reshape(bf16[4096,768]{0,1:T(8,128)(2,1)} %copy.101) | data formatting | bytes 12582912 | tf_op jit(solution)/shard_map/reshape | solution.py:194
  107.7 5.4 fusion.74
  114.7 54.4 %all-gather.13.cloned.1.call-done = bf16[4096,768]{0,1:T(8,128)(2,1)} async-done(((bf16[128,768]{0,1:T(8,128)(2,1)}), bf16[4096,768]{0,1:T(8,128)(2,1)}) %all-gather.13.cloned.1.call-update) | async-done | bytes 6291472 | tf_op jit(solution)/shard_map/all_gather | solution.py:193
  169.1 11.0 %reshape.260 = bf16[8,4,128,3,256]{2,1,0,4,3:T(4,128)(2,1)} reshape(bf16[4096,768]{0,1:T(8,128)(2,1)} %all-gather.13.cloned.1.call-done) | data formatting | bytes 12582912 | tf_op jit(solution)/shard_map/reshape | solution.py:194
  180.1 3.9 copy.206
  184.0 1.8 fusion.73
  187.9 2.5 copy-done.8
  190.4 5.1 convolution_convert_fusion.k
  195.5 2.3 add_convert_fusion.5.q
  197.7 5.6 add_convert_fusion.v
  203.3 12.0 %attend.1 = (bf16[512,1024]{1,0:T(8,128)(2,1)}, f32[8,512]{1,0:T(8,128)}) custom-call(s32[2,2]{1,0:T(2,128)} %pad_add_fusion.rng, s32[512,1]{1,0:T(8,128)} %copy.105.segq, s32[1,1536]{1,0:T(1,128)} %broadcast_in_dim.15.segk, bf16[512,1024]{1,0:T(8,128)(2,1)} %add_convert_fusion.5.q, bf16[1536,1024]{1,0:T(8,128)(2,1)} %convolution_convert_fusion.k, ...), custom_call_target="tpu_custom_call" | custom-call | tf_op jit(solution)/shard_map/attend/pallas_call | solution.py:102
  215.3 3.3 fusion.78
  219.0 1.9 copy-done.18
  220.9 6.6 %multiply_convert_fusion = (bf16[512,1024]{1,0:T(8,128)(2,1)}, f32[512,1024]{1,0:T(8,128)S(1)}, f32[512,1024]{1,0:T(8,128)S(1)}) fusion(f32[1024]{0:T(1024)S(1)} %bitcast.250, bf16[128,8,8,128]{3,2,1,0:T(8,128)(2,1)S(1)} %bitcast.228, f32[512,1024]{1,0:T(8,128)S(1)} %get-tuple-element.139, f32[1024]{0:T(1024)S(1)} %copy-done.33, f32[1024]{0:T(1024)S(1)} %copy-done.28, ...), kind=kOutput, calls=%fused_computation.61 | convolution fusion | flops 1110966272 | bytes 9453568 | tf_op jit(solution)/shard_map/dot_general | solution.py:21
  227.5 2.0 convert_reduce_fusion.3
  229.5 3.0 multiply_reduce_fusion.1
  232.5 3.0 convolution_convert_fusion.1
  235.6 3.3 stack.91
  238.9 2.6 copy.116
  241.6 2.8 convert_bitcast_fusion
  245.1 1.8 copy.117
  249.3 2.7 convolution_convert_fusion.2
  252.0 4.6 stack.90
  256.6 4.2 copy.115
  260.8 6.4 %pad_maximum_fusion.1 = bf16[3,8,128,4,256]{2,4,0,3,1:T(8,128)(2,1)} fusion(bf16[1,8,128,4,256]{2,4,0,3,1:T(8,128)(2,1)} %copy.117, bf16[1,8,128,4,256]{2,4,0,3,1:T(8,128)(2,1)} %copy.116, bf16[1,8,128,4,256]{2,4,0,3,1:T(8,128)(2,1)} %copy.115), kind=kLoop, calls=%fused_computation.1 | loop fusion | flops 6291456 | bytes 12582912 | tf_op jit(solution)/shard_map/stack | solution.py:202
  268.5 3.0 fusion.49.do
  272.4 1.8 copy.131
  274.2 2.6 reduce_sum.191
  277.5 25.7 %attend_back.1 = (bf16[512,1024]{1,0:T(8,128)(2,1)}, bf16[1536,1024]{1,0:T(8,128)(2,1)}, bf16[1536,1024]{1,0:T(8,128)(2,1)}) custom-call(s32[2,2]{1,0:T(2,128)} %pad_add_fusion.rng, s32[1,512]{1,0:T(1,128)} %bitcast.233, s32[1536,1]{1,0:T(8,128)} %broadcast_in_dim.18.segk, f32[8,512]{1,0:T(8,128)} %get-tuple-element.23.lse, f32[8,512]{1,0:T(8,128)} %bitcast.231, ...), custom_call_target="tpu_custom_call" | custom-call | tf_op jit(solution)/shard_map/attend_back/pallas_call | solution.py:163
  303.2 6.6 %convolution_convert_fusion.4 = bf16[1024,1024]{1,0:T(8,128)(2,1)} fusion(bf16[1536,1024]{1,0:T(8,128)(2,1)S(1)} %copy-done.9, bf16[1536,1024]{1,0:T(8,128)(2,1)} %get-tuple-element.24), kind=kOutput, calls=%fused_computation.82 | convolution fusion | flops 3222274048 | bytes 8388608 | tf_op jit(solution)/shard_map/dot_general | solution.py:29
  309.8 4.5 stack.87
  314.3 4.3 copy.111
  318.6 4.1 convolution_convert_fusion.5
  322.7 4.5 stack.86
  327.3 4.3 copy.110
  331.5 7.7 %convolution_convert_fusion.3 = bf16[1024,1024]{1,0:T(8,128)(2,1)} fusion(bf16[1536,1024]{1,0:T(8,128)(2,1)} %get-tuple-element.116, bf16[1536,1024]{1,0:T(8,128)(2,1)} %get-tuple-element.25), kind=kOutput, calls=%fused_computation.81 | convolution fusion | flops 3222274048 | bytes 8388608 | tf_op jit(solution)/shard_map/dot_general | solution.py:29
  339.2 4.5 stack.88
  343.7 4.3 copy.112
  348.0 6.5 %pad_maximum_fusion = bf16[3,8,128,4,256]{2,4,0,3,1:T(8,128)(2,1)} fusion(bf16[1,8,128,4,256]{2,4,0,3,1:T(8,128)(2,1)} %copy.112, bf16[1,8,128,4,256]{2,4,0,3,1:T(8,128)(2,1)} %copy.111, bf16[1,8,128,4,256]{2,4,0,3,1:T(8,128)(2,1)} %copy.110), kind=kLoop, calls=%fused_computation | loop fusion | flops 6291456 | bytes 12582912 | tf_op jit(solution)/shard_map/stack | solution.py:202
  355.1 66.6 %reduce-scatter.5.cloned.1.call-done = bf16[1,4,128,768]{2,3,1,0:T(8,128)(2,1)} async-done(((bf16[8,4,128,768]{2,3,1,0:T(8,128)(2,1)}), bf16[1,4,128,768]{2,3,1,0:T(8,128)(2,1)}) %reduce-scatter.5.cloned.1.call-update) | async-done | bytes 786448 | tf_op jit(solution)/shard_map/reduce_scatter | solution.py:204
  421.8 25.4 %reduce-scatter.11.cloned.1.call-done = bf16[1,1,128,768]{2,3,1,0:T(8,128)(2,1)} async-done(((bf16[1,4,128,768]{2,3,1,0:T(8,128)(2,1)}), bf16[1,1,128,768]{2,3,1,0:T(8,128)(2,1)}) %reduce-scatter.11.cloned.1.call-update) | async-done | bytes 196624 | tf_op jit(solution)/shard_map/reduce_scatter | solution.py:205
  449.3 6.1 %fusion.15 = f32[1536,1024]{1,0:T(8,128)S(1)} fusion(bf16[1536,1024]{1,0:T(8,128)(2,1)} %get-tuple-element.24, bf16[128,8,8,128]{3,2,1,0:T(8,128)(2,1)} %bitcast.223), kind=kOutput, calls=%fused_computation.30 | convolution fusion | flops 3221225472 | bytes 11534336 | tf_op jit(solution)/shard_map/dot_general | solution.py:25
  455.5 5.7 fusion.79
  463.9 5.5 collective-permute-start.3
  469.4 4.8 add_convert_fusion.3
  479.0 2.5 convert_reduce_fusion
  481.5 10.8 %collective-permute-done.2 = bf16[512,1024]{1,0:T(8,128)(2,1)} collective-permute-done((bf16[512,1024]{1,0:T(8,128)(2,1)}, bf16[512,1024]{1,0:T(8,128)(2,1)}, u32[]{:S(2)}, u32[]{:S(2)}) %collective-permute-start.2) | collective-permute-done | bytes 1048608 | tf_op jit(solution)/shard_map/ppermute | solution.py:185
  492.3 6.1 %multiply_reduce_fusion.2 = (f32[1024]{0:T(1024)S(1)}, f32[512]{0:T(512)S(1)}, f32[512]{0:T(512)S(1)}, f32[1024]{0:T(1024)S(1)}, f32[512,1024]{1,0:T(8,128)}) fusion(f32[1536,1024]{1,0:T(8,128)} %get-tuple-element.115, f32[1024]{0:T(1024)S(1)} %copy-done.25, bf16[512,1024]{1,0:T(8,128)(2,1)} %collective-permute-done.3, ...), kind=kOutput, calls=%fused_computation.55 | convolution fusion | flops 1080030208 | bytes 11550720 | tf_op jit(solution)/shard_map/dot_general | solution.py:25
  498.5 40.4 %psum.7 = f32[9,1024]{1,0:T(8,128)S(1)} all-reduce(f32[9,1024]{1,0:T(8,128)S(1)} %stack.85), channel_id=1, replica_groups=mesh['seq'=8,'tp'=4] {'seq','tp'}, use_global_device_ids=true, to_apply=%region_20.21 | all-reduce | flops 9216 | bytes 73728 | tf_op jit(solution)/shard_map/psum | solution.py:322
  541.2 3.7 add_convert_fusion.2
  544.9 3.1 copy.119
  548.1 4.6 reshape.265
  552.6 3.5 slice_bitcast_fusion
  557.5 3.1 copy.114
  560.6 4.6 reshape.264
  565.2 3.1 slice_bitcast_fusion.2
  568.3 2.5 copy.123
  (145 shorter events, 37.4 us)
Async XLA Ops:
  7.2 1.1 copy-start
  7.2 5.3 copy-start.2
  7.2 12.3 %copy-start.26 = (s32[1,2048]{1,0:T(1,128)S(1)}, s32[1,2048]{1,0:T(1,128)}, u32[]{:S(2)}) copy-start(s32[1,2048]{1,0:T(1,128)} %param.20) | copy-start | bytes 24580
  7.2 14.1 %copy-start.29 = (f32[256]{0:T(256)S(1)}, f32[256]{0:T(256)}, u32[]{:S(2)}) copy-start(f32[256]{0:T(256)} %param.34) | copy-start | bytes 3076
  7.2 14.0 %copy-start.30 = (f32[256]{0:T(256)S(1)}, f32[256]{0:T(256)}, u32[]{:S(2)}) copy-start(f32[256]{0:T(256)} %param.28) | copy-start | bytes 3076
  7.2 14.0 %copy-start.31 = (f32[256]{0:T(256)S(1)}, f32[256]{0:T(256)}, u32[]{:S(2)}) copy-start(f32[256]{0:T(256)} %param.27) | copy-start | bytes 3076
  7.3 80.7 %all-gather.11.cloned.1.call-start = ((), (), s32[]{:S(2)}) async-start(), calls=%async_computation.10 | async-start | bytes 6488064 | tf_op jit(solution)/shard_map/all_gather | solution.py:193
  9.8 159.2 %all-gather.13.cloned.1.call-start = ((), (), s32[]{:S(2)}) async-start(), calls=%async_computation.11 | async-start | bytes 6488064 | tf_op jit(solution)/shard_map/all_gather | solution.py:193
  12.5 342.1 %reduce-scatter.9.cloned.1.call-start = ((), (), s32[]{:S(2)}) async-start(), calls=%async_computation.7 | async-start | bytes 7077888 | tf_op jit(solution)/shard_map/reduce_scatter | solution.py:204
  12.5 51.8 %collective-permute-start = (bf16[512,1024]{1,0:T(8,128)(2,1)S(1)}, bf16[512,1024]{1,0:T(8,128)(2,1)S(1)}, u32[]{:S(2)}, u32[]{:S(2)}) collective-permute-start(bf16[512,1024]{1,0:T(8,128)(2,1)S(1)} %copy-done.2), channel_id=1, source_target_pairs={{0,1},{1,2},{2,3},{4,5},{5,6},{6,7},{8,9},{9,10},{10,11},{12,13},{... | collective-permute-start | bytes 3145736 | tf_op jit(solution)/shard_map/ppermute | solution.py:185
  17.5 46.8 %collective-permute-start.1 = (bf16[512,1024]{1,0:T(8,128)(2,1)S(1)}, bf16[512,1024]{1,0:T(8,128)(2,1)}, u32[]{:S(2)}, u32[]{:S(2)}) collective-permute-start(bf16[512,1024]{1,0:T(8,128)(2,1)S(1)} %copy-done.2), channel_id=1, source_target_pairs={{1,0},{2,1},{3,2},{5,4},{6,5},{7,6},{9,8},{10,9},{11,10},{13,12},{... | collective-permute-start | bytes 3145736 | tf_op jit(solution)/shard_map/ppermute | solution.py:185
  19.6 49.3 %copy-start.24 = (s32[512]{0:T(512)}, s32[512]{0:T(512)S(1)}, u32[]{:S(2)}) copy-start(s32[512]{0:T(512)S(1)} %slice.146) | copy-start | bytes 6148
  69.0 4.7 copy-start.25
  69.0 4.7 copy-start.27
  184.0 2.0 copy-start.5
  185.7 29.6 %copy-start.17 = (bf16[1,8,128,4,256]{2,1,4,3,0:T(8,128)(2,1)}, bf16[1,8,128,4,256]{2,1,4,3,0:T(8,128)(2,1)S(1)}, u32[]{:S(2)}) copy-start(bf16[1,8,128,4,256]{2,1,4,3,0:T(8,128)(2,1)S(1)} %get-tuple-element.111) | copy-start | bytes 6291460
  185.7 41.8 %copy-start.16 = (bf16[1,8,128,4,256]{2,1,4,3,0:T(8,128)(2,1)}, bf16[1,8,128,4,256]{2,1,4,3,0:T(8,128)(2,1)S(1)}, u32[]{:S(2)}) copy-start(bf16[1,8,128,4,256]{2,1,4,3,0:T(8,128)(2,1)S(1)} %get-tuple-element.109) | copy-start | bytes 6291460
  186.2 1.7 copy-start.15
  186.2 4.1 copy-start.8
  186.5 9.0 %copy-start.11 = (bf16[1,8,128,4,256]{2,1,4,3,0:T(8,128)(2,1)}, bf16[1,8,128,4,256]{2,1,4,3,0:T(8,128)(2,1)S(1)}, u32[]{:S(2)}) copy-start(bf16[1,8,128,4,256]{2,1,4,3,0:T(8,128)(2,1)S(1)} %copy.102) | copy-start | bytes 6291460
  195.5 2.3 copy-start.13
  203.3 12.0 %copy-start.32 = (f32[1024]{0:T(1024)S(1)}, f32[1024]{0:T(1024)}, u32[]{:S(2)}) copy-start(f32[1024]{0:T(1024)} %param.30) | copy-start | bytes 12292
  218.5 14.0 %copy-start.3 = (f32[512,1024]{1,0:T(8,128)}, f32[512,1024]{1,0:T(8,128)S(1)}, u32[]{:S(2)}) copy-start(f32[512,1024]{1,0:T(8,128)S(1)} %get-tuple-element.139) | copy-start | bytes 6291460
  218.6 2.3 copy-start.18
  218.6 2.3 copy-start.28
  218.6 2.3 copy-start.33
  220.9 6.6 %copy-start.19 = (bf16[512,1024]{1,0:T(8,128)(2,1)S(1)}, bf16[512,1024]{1,0:T(8,128)(2,1)}, u32[]{:S(2)}) copy-start(bf16[512,1024]{1,0:T(8,128)(2,1)} %param.37) | copy-start | bytes 3145732
  244.4 2.5 copy-start.20
  245.0 1.9 copy-start.4
  245.1 3.1 copy-start.10
  248.1 1.2 copy-start.22
  267.3 154.5 %reduce-scatter.5.cloned.1.call-start = ((), (), s32[]{:S(2)}) async-start(), calls=%async_computation.4 | async-start | bytes 7077888 | tf_op jit(solution)/shard_map/reduce_scatter | solution.py:204
  268.5 3.0 copy-start.23
  271.4 1.0 copy-start.6
  277.5 25.7 %copy-start.9 = (bf16[1536,1024]{1,0:T(8,128)(2,1)S(1)}, bf16[1536,1024]{1,0:T(8,128)(2,1)}, u32[]{:S(2)}) copy-start(bf16[1536,1024]{1,0:T(8,128)(2,1)} %get-tuple-element.116) | copy-start | bytes 9437188
  354.5 92.7 %reduce-scatter.11.cloned.1.call-start = ((), (), s32[]{:S(2)}) async-start(), calls=%async_computation.8 | async-start | bytes 983040 | tf_op jit(solution)/shard_map/reduce_scatter | solution.py:205
  355.1 120.6 %reduce-scatter.7.cloned.1.call-start = ((), (), s32[]{:S(2)}) async-start(), calls=%async_computation.5 | async-start | bytes 983040 | tf_op jit(solution)/shard_map/reduce_scatter | solution.py:205
  421.7 123.2 %all-gather.9.cloned.1.call-start = ((), (), s32[]{:S(2)}) async-start(), calls=%async_computation.9 | async-start | bytes 1769472 | tf_op jit(solution)/shard_map/all_gather | solution.py:206
  449.0 108.5 %all-gather.7.cloned.1.call-start = ((), (), s32[]{:S(2)}) async-start(), calls=%async_computation.6 | async-start | bytes 1769472 | tf_op jit(solution)/shard_map/all_gather | solution.py:206
  449.3 6.2 %copy-start.7 = (bf16[1536,1024]{1,0:T(8,128)(2,1)S(1)}, bf16[1536,1024]{1,0:T(8,128)(2,1)}, u32[]{:S(2)}) copy-start(bf16[1536,1024]{1,0:T(8,128)(2,1)} %get-tuple-element.25) | copy-start | bytes 9437188
  449.3 6.2 %copy-start.14 = (bf16[1,8,128,4,256]{2,1,4,3,0:T(8,128)(2,1)S(1)}, bf16[1,8,128,4,256]{2,1,4,3,0:T(8,128)(2,1)}, u32[]{:S(2)}) copy-start(bf16[1,8,128,4,256]{2,1,4,3,0:T(8,128)(2,1)} %copy.104) | copy-start | bytes 6291460
  461.1 8.3 %copy-start.34 = (f32[1024]{0:T(1024)S(1)}, f32[1024]{0:T(1024)}, u32[]{:S(2)}) copy-start(f32[1024]{0:T(1024)} %param.36) | copy-start | bytes 12292
  462.6 29.6 %collective-permute-start.2 = (bf16[512,1024]{1,0:T(8,128)(2,1)}, bf16[512,1024]{1,0:T(8,128)(2,1)}, u32[]{:S(2)}, u32[]{:S(2)}) collective-permute-start(bf16[512,1024]{1,0:T(8,128)(2,1)} %get-tuple-element.123), channel_id=1, source_target_pairs={{1,0},{2,1},{3,2},{5,4},{6,5},{7,6},{9,8},{10,9},{11,10},{13,12},{... | collective-permute-start | bytes 3145736 | tf_op jit(solution)/shard_map/ppermute | solution.py:185
  463.9 28.3 %collective-permute-start.3 = (bf16[512,1024]{1,0:T(8,128)(2,1)}, bf16[512,1024]{1,0:T(8,128)(2,1)}, u32[]{:S(2)}, u32[]{:S(2)}) collective-permute-start(bf16[512,1024]{1,0:T(8,128)(2,1)} %get-tuple-element.124), channel_id=1, source_target_pairs={{0,1},{1,2},{2,3},{4,5},{5,6},{6,7},{8,9},{9,10},{10,11},{12,13},{... | collective-permute-start | bytes 3145736 | tf_op jit(solution)/shard_map/ppermute | solution.py:185
  477.4 14.8 %copy-start.12 = (bf16[1,8,128,4,256]{2,1,4,3,0:T(8,128)(2,1)S(1)}, bf16[1,8,128,4,256]{2,1,4,3,0:T(8,128)(2,1)}, u32[]{:S(2)}) copy-start(bf16[1,8,128,4,256]{2,1,4,3,0:T(8,128)(2,1)} %copy-done.11) | copy-start | bytes 6291460
  477.4 14.8 %copy-start.21 = (bf16[512,1024]{1,0:T(8,128)(2,1)S(1)}, bf16[512,1024]{1,0:T(8,128)(2,1)}, u32[]{:S(2)}) copy-start(bf16[512,1024]{1,0:T(8,128)(2,1)} %get-tuple-element.26) | copy-start | bytes 3145732
  570.8 2.6 copy-start.1
Sparse Core Ops, SparseCore 0:
  11.5 76.3 all-gather.10
  91.4 77.6 all-gather.12
  267.4 61.7 reduce-scatter.8
  354.6 67.0 reduce-scatter.4
  423.9 23.2 reduce-scatter.10
  449.4 26.2 reduce-scatter.6
  478.1 24.5 all-gather.8
  505.2 25.7 all-gather.6
